TPU v7x, 768 devices: a whole 4x8x12 slice. The times are simulated.
768 devices in a mesh: seq: 48 (over z, y_lo, core), head: 16 (over y_hi, x).
Axes of the slice: x: 4, y: 8 (y_hi: 4, y_lo: 2; y = y_hi * 2 + y_lo), z: 12, core: 2. Of those that a mesh axis runs over, the one named last changes fastest.
Arguments:
- queries: float32 [12288, 16, 256], P('seq', 'head'), may hold values from -6 to 6
- key_rows: float32 [12288, 256], P(('seq', 'head')), may hold values from -6 to 6
- value_rows: float32 [12288, 256], P(('seq', 'head')), may hold values from -6 to 6
- forward_out: float32 [12288, 16, 256], P('seq', 'head'), may hold values from -6 to 6
- out_grad: float32 [12288, 16, 256], P('seq', 'head'), may hold values from -6 to 6
- log_norm: float32 [12288, 16], P('seq', 'head'), may hold values from 6 to 9
- doc_ids: int32 [12288], P(('seq', 'head')), may hold values from 0 to 5, never falling along the last dimension, each value on 1 to 4096 neighbouring positions
Outputs:
- grad_queries: float32 [12288, 16, 256], P('seq', 'head')
- grad_keys: float32 [12288, 256], P(('seq', 'head'))
- grad_values: float32 [12288, 256], P(('seq', 'head'))
Inputs may be any that keep to these rules, and one draw needn't show every extreme that they name: `doc_ids`: never falling along the tokens; each document holds 1 to 4096 tokens, one exactly 4096.
All inputs are finite; a program needn't handle non-finite values.
Results may differ from a plain program's by a relative error of at most 0.0003.
Values sent between devices are 32-bit elements; how exact they have to be, the bound alone decides.
A program may use at most 64 MiB of HBM per device.

v0:
```python
import jax
import jax.numpy as jnp
from jax import lax
from jax.sharding import PartitionSpec as P

WIN = 2048


def shifted(value, axis, steps):
    count = lax.axis_size(axis)
    leading, last = (max(0, -steps), min(count, count - steps))
    return lax.ppermute(value, axis, [(source, source + steps) for source in range(leading, last)])


def sent_together(arrays, axis, dim, along):
    columns = [a.reshape(*a.shape[:along], -1) for a in arrays]
    both = jnp.concatenate(columns, axis=along)
    whole, at, gathered = (lax.all_gather(both, axis, axis=dim, tiled=True), 0, [])
    for a, column in zip(arrays, columns):
        piece = whole[..., at : at + column.shape[along]]
        gathered.append(piece.reshape(*piece.shape[:along], *a.shape[along:]))
        at += column.shape[along]
    return tuple(gathered)


def side_by_side(arrays, axis, dim, along):
    widths = [a.shape[along] for a in arrays]
    both = jnp.concatenate(arrays, axis=along)
    whole = lax.psum_scatter(both, axis, scatter_dimension=dim, tiled=True)
    return tuple(jnp.split(whole, [sum(widths[:k]) for k in range(1, len(widths))], axis=along))


def on_device(queries, key_rows, value_rows, forward_out, out_grad, log_norm, doc_ids):
    row_count, local_heads, head_width = queries.shape
    reach = WIN // row_count
    factor = head_width ** (-0.5)
    high = lax.Precision.HIGHEST
    id_float = doc_ids.astype(jnp.float32)
    key_parts = []
    val_parts = []
    id_parts = []
    for distance in range(reach, 0, -1):
        far_keys, far_vals, far_ids = shifted((key_rows, value_rows, id_float), "seq", distance)
        key_parts.append(far_keys)
        val_parts.append(far_vals)
        id_parts.append(far_ids)
    key_stack = jnp.stack(key_parts + [key_rows], axis=0)
    val_stack = jnp.stack(val_parts + [value_rows], axis=0)
    id_stack = jnp.stack(id_parts + [id_float], axis=0)
    key_stack, val_stack, id_stack = sent_together((key_stack, val_stack, id_stack), "head", 1, 2)
    key_window = key_stack.reshape(-1, head_width)
    val_window = val_stack.reshape(-1, head_width)
    id_window = id_stack.reshape(-1)
    extent = key_window.shape[0]
    query_ids = id_window[extent - row_count :]
    first_row = lax.axis_index("seq") * row_count
    query_pos = first_row + jnp.arange(row_count, dtype=jnp.int32)
    key_pos = first_row - reach * row_count + jnp.arange(extent, dtype=jnp.int32)
    spacing = query_pos[:, None] - key_pos[None, :]
    allowed = (
        (spacing >= 0)
        & (spacing < WIN)
        & (query_ids[:, None] == id_window[None, :])
        & (key_pos[None, :] >= 0)
    )
    scores = jnp.einsum("rhd,kd->hrk", queries, key_window, precision=high) * factor
    probs = jnp.where(allowed[None], jnp.exp(scores - log_norm.T[:, :, None]), 0.0)
    vals_grad = jnp.einsum("hrk,rhd->kd", probs, out_grad, precision=high)
    grad_probs = jnp.einsum("rhd,kd->hrk", out_grad, val_window, precision=high)
    delta = jnp.sum(out_grad * forward_out, axis=-1)
    grad_scores = probs * (grad_probs - delta.T[:, :, None])
    grad_queries = jnp.einsum("hrk,kd->rhd", grad_scores, key_window, precision=high) * factor
    keys_grad = jnp.einsum("hrk,rhd->kd", grad_scores, queries, precision=high) * factor
    kgrad_stack = keys_grad.reshape(reach + 1, row_count, head_width)
    vgrad_stack = vals_grad.reshape(reach + 1, row_count, head_width)
    kgrad_stack, vgrad_stack = side_by_side((kgrad_stack, vgrad_stack), "head", 1, 0)
    grad_keys = kgrad_stack[reach]
    grad_values = vgrad_stack[reach]
    for distance in range(1, reach + 1):
        back_keys, back_vals = shifted(
            (kgrad_stack[reach - distance], vgrad_stack[reach - distance]), "seq", -distance
        )
        grad_keys = grad_keys + back_keys
        grad_values = grad_values + back_vals
    return (grad_queries, grad_keys, grad_values)


def solution(mesh):
    in_specs = (
        P("seq", "head", None),
        P(("seq", "head"), None),
        P(("seq", "head"), None),
        P("seq", "head", None),
        P("seq", "head", None),
        P("seq", "head"),
        P(("seq", "head")),
    )
    out_specs = (P("seq", "head", None), P(("seq", "head"), None), P(("seq", "head"), None))
    return jax.shard_map(
        on_device, mesh=mesh, in_specs=in_specs, out_specs=out_specs, check_vma=False
    )
```

profile of v0, /device:TPU:704, one launch (start us, length us, event | category | flops | bytes accessed | tf_op | source)
XLA Modules:
  0.0 364.7 jit_solution(14969309140950404754)
XLA Ops:
  17.4 1.9 collective-permute-start.21
  22.9 1.9 collective-permute-start.23
  33.1 2.8 collective-permute-start.14
  35.9 1.9 collective-permute-start.15
  45.1 3.0 collective-permute-done
  50.0 1.9 collective-permute-start.6
  52.0 1.9 collective-permute-start.7
  54.0 2.8 collective-permute-done.6
  59.8 2.1 multiply_reduce_fusion
  61.8 113.5 %all-gather.2.cloned.1.call-done = f32[9,256,513]{2,1,0:T(8,128)} async-done(((f32[9,16,513]{2,1,0:T(8,128)}), f32[9,256,513]{2,1,0:T(8,128)}) %all-gather.2.cloned.1.call-update) | async-done | bytes 4727824 | tf_op jit(solution)/shard_map/all_gather | solution.py:18
  177.0 2.8 fusion.38
  181.0 2.9 fusion.4
  183.9 2.1 fusion.13
  186.0 2.1 fusion.8
  188.2 2.1 convolution_multiply_fusion
  190.3 2.6 pad_maximum_fusion
  192.9 113.1 %reduce-scatter.2.cloned.1.call-done = f32[18,16,256]{2,1,0:T(8,128)} async-done(((f32[18,256,256]{2,1,0:T(8,128)}), f32[18,16,256]{2,1,0:T(8,128)}) %reduce-scatter.2.cloned.1.call-update) | async-done | bytes 294928 | tf_op jit(solution)/shard_map/reduce_scatter | solution.py:29
  306.9 3.9 %collective-permute-start.39 = (f32[16,256]{1,0:T(8,128)S(1)}, f32[16,256]{1,0:T(8,128)S(1)}, u32[]{:S(2)}, u32[]{:S(2)}) collective-permute-start(f32[16,256]{1,0:T(8,128)S(1)} %get-tuple-element.14), channel_id=1, source_target_pairs={{128,0},{144,16},{160,32},{176,48},{192,64},{208,80},{224,96},{240... | collective-permute-start | bytes 49160 | tf_op jit(solution)/shard_map/ppermute | solution.py:12
  310.8 2.5 collective-permute-start.38
  313.3 4.2 %collective-permute-start.37 = (f32[16,256]{1,0:T(8,128)S(1)}, f32[16,256]{1,0:T(8,128)S(1)}, u32[]{:S(2)}, u32[]{:S(2)}) collective-permute-start(f32[16,256]{1,0:T(8,128)S(1)} %get-tuple-element.16), channel_id=1, source_target_pairs={{96,0},{112,16},{128,32},{144,48},{160,64},{176,80},{192,96},{208,... | collective-permute-start | bytes 49160 | tf_op jit(solution)/shard_map/ppermute | solution.py:12
  317.4 3.7 %collective-permute-start.36 = (f32[16,256]{1,0:T(8,128)S(1)}, f32[16,256]{1,0:T(8,128)S(1)}, u32[]{:S(2)}, u32[]{:S(2)}) collective-permute-start(f32[16,256]{1,0:T(8,128)S(1)} %get-tuple-element.17), channel_id=1, source_target_pairs={{80,0},{96,16},{112,32},{128,48},{144,64},{160,80},{176,96},{192,1... | collective-permute-start | bytes 49160 | tf_op jit(solution)/shard_map/ppermute | solution.py:12
  321.1 2.3 collective-permute-start.35
  323.5 1.9 collective-permute-start.34
  325.4 3.2 collective-permute-start.33
  328.7 3.2 collective-permute-start.32
  331.9 2.0 collective-permute-start.31
  335.2 2.8 collective-permute-start.29
  338.1 2.3 collective-permute-start.28
  342.2 1.9 collective-permute-start.26
  344.2 3.0 collective-permute-start.25
  347.2 2.8 collective-permute-start.24
  350.1 5.5 %fusion.12 = f32[256,1,256]{0,2,1:T(8,128)S(1)} fusion(f32[2304,256]{1,0:T(8,128)} %bitcast.178, f32[256,2304]{0,1:T(8,128)S(1)} %fusion.8), kind=kOutput, calls=%fused_computation.20 | convolution fusion | flops 1812004864 | bytes 4980736 | tf_op jit(solution)/shard_map/hrk,kd->rhd/dot_general | solution.py:72
  (101 shorter events, 43.1 us)
Async XLA Ops:
  7.2 168.1 %all-gather.2.cloned.1.call-start = ((), (), s32[]{:S(2)}) async-start(), calls=%async_computation.1 | async-start | bytes 6266880 | tf_op jit(solution)/shard_map/all_gather | solution.py:18
  7.2 23.1 %collective-permute-start.8 = (f32[16,256]{1,0:T(8,128)}, f32[16,256]{1,0:T(8,128)S(1)}, u32[]{:S(2)}, u32[]{:S(2)}) collective-permute-start(f32[16,256]{1,0:T(8,128)} %param.9), channel_id=1, source_target_pairs={{0,128},{16,144},{32,160},{48,176},{64,192},{80,208},{96,224},{112... | collective-permute-start | bytes 49160 | tf_op jit(solution)/shard_map/ppermute | solution.py:12
  11.8 9.2 %collective-permute-start.18 = (f32[16]{0:T(128)S(1)}, f32[16]{0:T(128)S(1)}, u32[]{:S(2)}, u32[]{:S(2)}) collective-permute-start(f32[16]{0:T(128)S(1)} %get-tuple-element.30), channel_id=1, source_target_pairs={{0,96},{16,112},{32,128},{48,144},{64,160},{80,176},{96,192},{112,... | collective-permute-start | bytes 200 | tf_op jit(solution)/shard_map/ppermute | solution.py:12
  13.1 9.9 %collective-permute-start.19 = (f32[16]{0:T(128)S(1)}, f32[16]{0:T(128)S(1)}, u32[]{:S(2)}, u32[]{:S(2)}) collective-permute-start(f32[16]{0:T(128)S(1)} %get-tuple-element.30), channel_id=1, source_target_pairs={{0,80},{16,96},{32,112},{48,128},{64,144},{80,160},{96,176},{112,1... | collective-permute-start | bytes 200 | tf_op jit(solution)/shard_map/ppermute | solution.py:12
  16.1 8.7 %collective-permute-start.20 = (f32[16]{0:T(128)S(1)}, f32[16]{0:T(128)S(1)}, u32[]{:S(2)}, u32[]{:S(2)}) collective-permute-start(f32[16]{0:T(128)S(1)} %get-tuple-element.30), channel_id=1, source_target_pairs={{0,64},{16,80},{32,96},{48,112},{64,128},{80,144},{96,160},{112,17... | collective-permute-start | bytes 200 | tf_op jit(solution)/shard_map/ppermute | solution.py:12
  17.4 8.7 %collective-permute-start.21 = (f32[16]{0:T(128)S(1)}, f32[16]{0:T(128)S(1)}, u32[]{:S(2)}, u32[]{:S(2)}) collective-permute-start(f32[16]{0:T(128)S(1)} %get-tuple-element.30), channel_id=1, source_target_pairs={{0,48},{16,64},{32,80},{48,96},{64,112},{80,128},{96,144},{112,160... | collective-permute-start | bytes 200 | tf_op jit(solution)/shard_map/ppermute | solution.py:12
  26.2 9.7 %collective-permute-start.10 = (f32[16,256]{1,0:T(8,128)}, f32[16,256]{1,0:T(8,128)S(1)}, u32[]{:S(2)}, u32[]{:S(2)}) collective-permute-start(f32[16,256]{1,0:T(8,128)} %param.9), channel_id=1, source_target_pairs={{0,96},{16,112},{32,128},{48,144},{64,160},{80,176},{96,192},{112,... | collective-permute-start | bytes 49160 | tf_op jit(solution)/shard_map/ppermute | solution.py:12
  27.5 10.3 %collective-permute-start.11 = (f32[16,256]{1,0:T(8,128)}, f32[16,256]{1,0:T(8,128)S(1)}, u32[]{:S(2)}, u32[]{:S(2)}) collective-permute-start(f32[16,256]{1,0:T(8,128)} %param.9), channel_id=1, source_target_pairs={{0,80},{16,96},{32,112},{48,128},{64,144},{80,160},{96,176},{112,1... | collective-permute-start | bytes 49160 | tf_op jit(solution)/shard_map/ppermute | solution.py:12
  28.8 10.3 %collective-permute-start.12 = (f32[16,256]{1,0:T(8,128)}, f32[16,256]{1,0:T(8,128)S(1)}, u32[]{:S(2)}, u32[]{:S(2)}) collective-permute-start(f32[16,256]{1,0:T(8,128)} %param.9), channel_id=1, source_target_pairs={{0,64},{16,80},{32,96},{48,112},{64,128},{80,144},{96,160},{112,17... | collective-permute-start | bytes 49160 | tf_op jit(solution)/shard_map/ppermute | solution.py:12
  30.3 10.2 %collective-permute-start.13 = (f32[16,256]{1,0:T(8,128)}, f32[16,256]{1,0:T(8,128)S(1)}, u32[]{:S(2)}, u32[]{:S(2)}) collective-permute-start(f32[16,256]{1,0:T(8,128)} %param.9), channel_id=1, source_target_pairs={{0,48},{16,64},{32,80},{48,96},{64,112},{80,128},{96,144},{112,160... | collective-permute-start | bytes 49160 | tf_op jit(solution)/shard_map/ppermute | solution.py:12
  37.8 10.3 %collective-permute-start = (f32[16,256]{1,0:T(8,128)}, f32[16,256]{1,0:T(8,128)S(1)}, u32[]{:S(2)}, u32[]{:S(2)}) collective-permute-start(f32[16,256]{1,0:T(8,128)} %param.8), channel_id=1, source_target_pairs={{0,128},{16,144},{32,160},{48,176},{64,192},{80,208},{96,224},{112... | collective-permute-start | bytes 49160 | tf_op jit(solution)/shard_map/ppermute | solution.py:12
  39.1 10.9 %collective-permute-start.1 = (f32[16,256]{1,0:T(8,128)}, f32[16,256]{1,0:T(8,128)S(1)}, u32[]{:S(2)}, u32[]{:S(2)}) collective-permute-start(f32[16,256]{1,0:T(8,128)} %param.8), channel_id=1, source_target_pairs={{0,112},{16,128},{32,144},{48,160},{64,176},{80,192},{96,208},{112... | collective-permute-start | bytes 49160 | tf_op jit(solution)/shard_map/ppermute | solution.py:12
  40.5 11.5 %collective-permute-start.2 = (f32[16,256]{1,0:T(8,128)}, f32[16,256]{1,0:T(8,128)S(1)}, u32[]{:S(2)}, u32[]{:S(2)}) collective-permute-start(f32[16,256]{1,0:T(8,128)} %param.8), channel_id=1, source_target_pairs={{0,96},{16,112},{32,128},{48,144},{64,160},{80,176},{96,192},{112,... | collective-permute-start | bytes 49160 | tf_op jit(solution)/shard_map/ppermute | solution.py:12
  41.8 12.2 %collective-permute-start.3 = (f32[16,256]{1,0:T(8,128)}, f32[16,256]{1,0:T(8,128)S(1)}, u32[]{:S(2)}, u32[]{:S(2)}) collective-permute-start(f32[16,256]{1,0:T(8,128)} %param.8), channel_id=1, source_target_pairs={{0,80},{16,96},{32,112},{48,128},{64,144},{80,160},{96,176},{112,1... | collective-permute-start | bytes 49160 | tf_op jit(solution)/shard_map/ppermute | solution.py:12
  43.1 10.9 %collective-permute-start.4 = (f32[16,256]{1,0:T(8,128)}, f32[16,256]{1,0:T(8,128)S(1)}, u32[]{:S(2)}, u32[]{:S(2)}) collective-permute-start(f32[16,256]{1,0:T(8,128)} %param.8), channel_id=1, source_target_pairs={{0,64},{16,80},{32,96},{48,112},{64,128},{80,144},{96,160},{112,17... | collective-permute-start | bytes 49160 | tf_op jit(solution)/shard_map/ppermute | solution.py:12
  59.7 246.3 %reduce-scatter.2.cloned.1.call-start = ((), (), s32[]{:S(2)}) async-start(), calls=%async_computation.2 | async-start | bytes 5013504 | tf_op jit(solution)/shard_map/reduce_scatter | solution.py:29
  306.9 16.5 %collective-permute-start.39 = (f32[16,256]{1,0:T(8,128)S(1)}, f32[16,256]{1,0:T(8,128)S(1)}, u32[]{:S(2)}, u32[]{:S(2)}) collective-permute-start(f32[16,256]{1,0:T(8,128)S(1)} %get-tuple-element.14), channel_id=1, source_target_pairs={{128,0},{144,16},{160,32},{176,48},{192,64},{208,80},{224,96},{240... | collective-permute-start | bytes 49160 | tf_op jit(solution)/shard_map/ppermute | solution.py:12
  310.8 14.6 %collective-permute-start.38 = (f32[16,256]{1,0:T(8,128)S(1)}, f32[16,256]{1,0:T(8,128)S(1)}, u32[]{:S(2)}, u32[]{:S(2)}) collective-permute-start(f32[16,256]{1,0:T(8,128)S(1)} %get-tuple-element.15), channel_id=1, source_target_pairs={{112,0},{128,16},{144,32},{160,48},{176,64},{192,80},{208,96},{224... | collective-permute-start | bytes 49160 | tf_op jit(solution)/shard_map/ppermute | solution.py:12
  313.3 15.4 %collective-permute-start.37 = (f32[16,256]{1,0:T(8,128)S(1)}, f32[16,256]{1,0:T(8,128)S(1)}, u32[]{:S(2)}, u32[]{:S(2)}) collective-permute-start(f32[16,256]{1,0:T(8,128)S(1)} %get-tuple-element.16), channel_id=1, source_target_pairs={{96,0},{112,16},{128,32},{144,48},{160,64},{176,80},{192,96},{208,... | collective-permute-start | bytes 49160 | tf_op jit(solution)/shard_map/ppermute | solution.py:12
  317.4 14.5 %collective-permute-start.36 = (f32[16,256]{1,0:T(8,128)S(1)}, f32[16,256]{1,0:T(8,128)S(1)}, u32[]{:S(2)}, u32[]{:S(2)}) collective-permute-start(f32[16,256]{1,0:T(8,128)S(1)} %get-tuple-element.17), channel_id=1, source_target_pairs={{80,0},{96,16},{112,32},{128,48},{144,64},{160,80},{176,96},{192,1... | collective-permute-start | bytes 49160 | tf_op jit(solution)/shard_map/ppermute | solution.py:12
  321.1 12.8 %collective-permute-start.35 = (f32[16,256]{1,0:T(8,128)S(1)}, f32[16,256]{1,0:T(8,128)S(1)}, u32[]{:S(2)}, u32[]{:S(2)}) collective-permute-start(f32[16,256]{1,0:T(8,128)S(1)} %get-tuple-element.18), channel_id=1, source_target_pairs={{64,0},{80,16},{96,32},{112,48},{128,64},{144,80},{160,96},{176,11... | collective-permute-start | bytes 49160 | tf_op jit(solution)/shard_map/ppermute | solution.py:12
  323.5 11.8 %collective-permute-start.34 = (f32[16,256]{1,0:T(8,128)S(1)}, f32[16,256]{1,0:T(8,128)S(1)}, u32[]{:S(2)}, u32[]{:S(2)}) collective-permute-start(f32[16,256]{1,0:T(8,128)S(1)} %get-tuple-element.19), channel_id=1, source_target_pairs={{48,0},{64,16},{80,32},{96,48},{112,64},{128,80},{144,96},{160,112... | collective-permute-start | bytes 49160 | tf_op jit(solution)/shard_map/ppermute | solution.py:12
  325.4 12.7 %collective-permute-start.33 = (f32[16,256]{1,0:T(8,128)S(1)}, f32[16,256]{1,0:T(8,128)S(1)}, u32[]{:S(2)}, u32[]{:S(2)}) collective-permute-start(f32[16,256]{1,0:T(8,128)S(1)} %get-tuple-element.20), channel_id=1, source_target_pairs={{32,0},{48,16},{64,32},{80,48},{96,64},{112,80},{128,96},{144,112}... | collective-permute-start | bytes 49160 | tf_op jit(solution)/shard_map/ppermute | solution.py:12
  328.7 11.7 %collective-permute-start.32 = (f32[16,256]{1,0:T(8,128)S(1)}, f32[16,256]{1,0:T(8,128)S(1)}, u32[]{:S(2)}, u32[]{:S(2)}) collective-permute-start(f32[16,256]{1,0:T(8,128)S(1)} %get-tuple-element.13), channel_id=1, source_target_pairs={{16,0},{32,16},{48,32},{64,48},{80,64},{96,80},{112,96},{128,112},... | collective-permute-start | bytes 49160 | tf_op jit(solution)/shard_map/ppermute | solution.py:12
  331.9 10.3 %collective-permute-start.31 = (f32[16,256]{1,0:T(8,128)S(1)}, f32[16,256]{1,0:T(8,128)S(1)}, u32[]{:S(2)}, u32[]{:S(2)}) collective-permute-start(f32[16,256]{1,0:T(8,128)S(1)} %get-tuple-element.21), channel_id=1, source_target_pairs={{128,0},{144,16},{160,32},{176,48},{192,64},{208,80},{224,96},{240... | collective-permute-start | bytes 49160 | tf_op jit(solution)/shard_map/ppermute | solution.py:12
  333.9 10.2 %collective-permute-start.30 = (f32[16,256]{1,0:T(8,128)S(1)}, f32[16,256]{1,0:T(8,128)S(1)}, u32[]{:S(2)}, u32[]{:S(2)}) collective-permute-start(f32[16,256]{1,0:T(8,128)S(1)} %get-tuple-element.22), channel_id=1, source_target_pairs={{112,0},{128,16},{144,32},{160,48},{176,64},{192,80},{208,96},{224... | collective-permute-start | bytes 49160 | tf_op jit(solution)/shard_map/ppermute | solution.py:12
  335.2 12.0 %collective-permute-start.29 = (f32[16,256]{1,0:T(8,128)S(1)}, f32[16,256]{1,0:T(8,128)S(1)}, u32[]{:S(2)}, u32[]{:S(2)}) collective-permute-start(f32[16,256]{1,0:T(8,128)S(1)} %get-tuple-element.23), channel_id=1, source_target_pairs={{96,0},{112,16},{128,32},{144,48},{160,64},{176,80},{192,96},{208,... | collective-permute-start | bytes 49160 | tf_op jit(solution)/shard_map/ppermute | solution.py:12
  338.1 18.4 %collective-permute-start.28 = (f32[16,256]{1,0:T(8,128)S(1)}, f32[16,256]{1,0:T(8,128)S(1)}, u32[]{:S(2)}, u32[]{:S(2)}) collective-permute-start(f32[16,256]{1,0:T(8,128)S(1)} %get-tuple-element.24), channel_id=1, source_target_pairs={{80,0},{96,16},{112,32},{128,48},{144,64},{160,80},{176,96},{192,1... | collective-permute-start | bytes 49160 | tf_op jit(solution)/shard_map/ppermute | solution.py:12
  340.4 16.0 %collective-permute-start.27 = (f32[16,256]{1,0:T(8,128)S(1)}, f32[16,256]{1,0:T(8,128)S(1)}, u32[]{:S(2)}, u32[]{:S(2)}) collective-permute-start(f32[16,256]{1,0:T(8,128)S(1)} %get-tuple-element.25), channel_id=1, source_target_pairs={{64,0},{80,16},{96,32},{112,48},{128,64},{144,80},{160,96},{176,11... | collective-permute-start | bytes 49160 | tf_op jit(solution)/shard_map/ppermute | solution.py:12
  342.2 14.2 %collective-permute-start.26 = (f32[16,256]{1,0:T(8,128)S(1)}, f32[16,256]{1,0:T(8,128)S(1)}, u32[]{:S(2)}, u32[]{:S(2)}) collective-permute-start(f32[16,256]{1,0:T(8,128)S(1)} %get-tuple-element.26), channel_id=1, source_target_pairs={{48,0},{64,16},{80,32},{96,48},{112,64},{128,80},{144,96},{160,112... | collective-permute-start | bytes 49160 | tf_op jit(solution)/shard_map/ppermute | solution.py:12
  344.2 12.3 %collective-permute-start.25 = (f32[16,256]{1,0:T(8,128)S(1)}, f32[16,256]{1,0:T(8,128)S(1)}, u32[]{:S(2)}, u32[]{:S(2)}) collective-permute-start(f32[16,256]{1,0:T(8,128)S(1)} %get-tuple-element.27), channel_id=1, source_target_pairs={{32,0},{48,16},{64,32},{80,48},{96,64},{112,80},{128,96},{144,112}... | collective-permute-start | bytes 49160 | tf_op jit(solution)/shard_map/ppermute | solution.py:12
  347.2 9.2 %collective-permute-start.24 = (f32[16,256]{1,0:T(8,128)S(1)}, f32[16,256]{1,0:T(8,128)S(1)}, u32[]{:S(2)}, u32[]{:S(2)}) collective-permute-start(f32[16,256]{1,0:T(8,128)S(1)} %get-tuple-element.28), channel_id=1, source_target_pairs={{16,0},{32,16},{48,32},{64,48},{80,64},{96,80},{112,96},{128,112},... | collective-permute-start | bytes 49160 | tf_op jit(solution)/shard_map/ppermute | solution.py:12
  (14 other events, 84.2 us)
Sparse Core Ops, SparseCore 0:
  59.8 115.4 all-gather.1
  193.0 112.9 reduce-scatter.1
where the time goes:
time: 366 us; the launch traced here: 365 us
  waiting for transfers between devices  238 us (65%)
  starting transfers between devices  80.4 us (22%)
  between operations  14.9 us (4%)
  matrix products  14.7 us (4%)
  local copies, waits for them, and re-layouts  9.07 us (2%)
  other arithmetic  7.49 us (2%)
    all_gather x1, waiting for transfers between devices, sent_together(): lax.all_gather(both, axis, axis=dim, tiled=True)  113 us
    reduce_scatter x1, waiting for transfers between devices, side_by_side(): whole = lax.psum_scatter(both, axis, scatter_dimension=dim, tiled=True)  113 us
    ppermute x40, starting transfers between devices, shifted(): lax.ppermute(value, axis, [(source, source + steps) for source in range(l...  80.3 us
    ppermute x40, waiting for transfers between devices, shifted(): lax.ppermute(value, axis, [(source, source + steps) for source in range(l...  11.5 us
  transfers between devices with their start and end apart: 42, of which 8 were waited for; matrix products, arithmetic and copies ran while one was open for 3% of the time, Pallas kernels for 0%

commit v1 on v0

v1 whole, which is shorter than its diff:
```python
import functools

import jax
import jax.numpy as jnp
from jax import lax
from jax.experimental import pallas as pl
from jax.experimental.pallas import tpu as pltpu
from jax.sharding import PartitionSpec as P

MESH = pl.DeviceIdType.MESH
WIN = 2048
ROWS = 256
PIECE = 16
UNITS = 5
NY = 4
BAND = NY * PIECE
KEYS = 9 * BAND
PAD = 640
f32, bf16 = jnp.float32, jnp.bfloat16


def halves(value):
    high = value.astype(bf16)
    return high, (value - high.astype(f32)).astype(bf16)


def dot(a, b, b_dim):
    return lax.dot_general(a, b, (((1,), (b_dim,)), ((), ())), preferred_element_type=f32)


def dot3(a_high, a_low, b_high, b_low, b_dim):
    return dot(a_high, b_high, b_dim) + dot(a_high, b_low, b_dim) + dot(a_low, b_high, b_dim)


def kernel(
    q_hbm, k_hbm, v_hbm, o_hbm, g_hbm, norm_hbm, ids_hbm,
    dq_out, dk_out, dv_out,
    qb, gb, st, fwd, norm_in, ids_in, k_in, v_in,
    kbuf, vbuf, idq,
    kf, kh, kl, vh, vl, kth, ktl, idk, bias,
    qh, ql, gh, gl, sh, sl,
    acc_k, acc_v, core_k, core_v, y_k, u_k, u_v, y_v, sum_k, sum_v, dq_part, dq_in,
    in_sem, x_send, x_recv, k_send, k_recv, v_send, v_recv, c_send, c_recv, r_send, r_recv,
):
    seq, head = lax.axis_index("seq"), lax.axis_index("head")
    n_seq = lax.axis_size("seq")
    unit, core = lax.div(seq, 2), lax.rem(seq, 2)
    n_unit = n_seq // 2
    yh, x = lax.div(head, 4), lax.rem(head, 4)
    other = 1 - core

    def at_unit(d):
        return (lax.rem(unit + d + n_unit, n_unit) * 2 + core, head)

    def at_y(d):
        return (seq, lax.rem(yh + d, NY) * 4 + x)

    def at_x(d):
        return (seq, yh * 4 + lax.rem(x + d + 4, 4))

    partner = (unit * 2 + other, head)

    def send(src, dst, s_sem, r_sem, to):
        copy = pltpu.make_async_remote_copy(
            src_ref=src, dst_ref=dst, send_sem=s_sem, recv_sem=r_sem, device_id=to, device_id_type=MESH
        )
        copy.start()
        started.append(copy)
        return copy

    def landed(dst, r_sem):
        pltpu.make_async_remote_copy(
            src_ref=dst, dst_ref=dst, send_sem=r_sem, recv_sem=r_sem, device_id=partner, device_id_type=MESH
        ).wait_recv()

    started = []

    loads = [
        pltpu.make_async_copy(src, dst, in_sem.at[i])
        for i, (src, dst) in enumerate(
            (
                (q_hbm, qb.at[0]), (k_hbm, k_in), (v_hbm, v_in), (ids_hbm, ids_in),
                (g_hbm, gb.at[0]), (o_hbm, fwd), (norm_hbm, norm_in),
            )
        )
    ]
    for load in loads:
        load.start()
    barrier = pltpu.get_barrier_semaphore()
    greeted = [at_x(1), at_x(-1), at_x(2), partner]
    greeted += [at_y(d) for d in (1, 2, 3)] + [at_unit(-d) for d in (1, 2, 3, 4)]
    for device in greeted:
        pl.semaphore_signal(barrier, inc=1, device_id=device, device_id_type=MESH)

    for load in loads[:4]:
        load.wait()
    ids_row = ids_in[...].astype(f32)
    across = lax.broadcasted_iota(jnp.int32, (8, PIECE), 1)
    down = lax.broadcasted_iota(jnp.int32, (8, PIECE), 0)
    ids_low = jnp.sum(jnp.where(across == down, ids_row, 0.0), axis=1, keepdims=True)
    ids_high = jnp.sum(jnp.where(across == down + 8, ids_row, 0.0), axis=1, keepdims=True)
    lane = lax.broadcasted_iota(jnp.int32, (8, 128), 1)
    ids_tile = jnp.where(lane < 64, ids_low, ids_high)
    mine_k = kbuf.at[4, core, yh]
    mine_v = vbuf.at[4, core, yh]
    kbuf[4, core, yh, 0:16, :] = k_in[:, :128]
    kbuf[4, core, yh, 16:32, :] = k_in[:, 128:]
    kbuf[4, core, yh, 32:40, :] = ids_tile
    vbuf[4, core, yh, 0:16, :] = v_in[:, :128]
    vbuf[4, core, yh, 16:32, :] = v_in[:, 128:]
    pl.semaphore_wait(barrier, len(greeted))

    q_right = send(qb.at[0], qb.at[1], x_send.at[0], x_recv.at[0], at_x(1))
    q_left = send(qb.at[0], qb.at[2], x_send.at[1], x_recv.at[1], at_x(-1))
    for d in (1, 2, 3):
        send(mine_k, mine_k, k_send.at[d - 1], k_recv.at[4, yh], at_y(d))
    for d in (1, 2, 3, 4):
        send(mine_v, vbuf.at[4 - d, core, yh], v_send.at[d - 1], v_recv.at[4 - d, yh], at_unit(d))
    for d in (1, 2, 3):
        send(mine_v, mine_v, v_send.at[d + 3], v_recv.at[4, yh], at_y(d))

    for load in loads[4:]:
        load.wait()
    product = gb[0] * fwd[...]
    fwd[...] = product
    folded = fwd[pl.ds(0, ROWS, stride=2), :] + fwd[pl.ds(1, ROWS, stride=2), :]
    st[0, 0:1, :] = norm_in[...]
    st[0, 1:2, :] = jnp.sum(folded.T, axis=0, keepdims=True)
    st[0, 2:8, :] = jnp.zeros((6, ROWS), f32)

    def ys(d):
        return lax.rem(yh + d, NY)

    for d in (1, 2, 3):
        landed(kbuf.at[4, core, ys(d)], k_recv.at[4, ys(d)])
    for d in (1, 2, 3, 4):
        send(kbuf.at[4, core], kbuf.at[4 - d, core], k_send.at[d + 2], k_recv.at[4 - d, 0], at_unit(d))
    idq[pl.ds(x, 1)] = kbuf[4, core, :, 32:40, :][None]
    for d in (1, 2, 3):
        send(idq.at[x], idq.at[x], x_send.at[d + 9], x_recv.at[d + 9], at_x(d))
    for d in (1, 2, 3, 4):
        landed(vbuf.at[4 - d, core, yh], v_recv.at[4 - d, yh])
    for d in (1, 2, 3):
        send(
            vbuf.at[pl.ds(0, 4), core, yh], vbuf.at[pl.ds(0, 4), core, yh],
            v_send.at[d + 6], v_recv.at[5, yh], at_y(d),
        )
    q_right.wait_send()
    q_left.wait_send()
    started.remove(q_right)
    started.remove(q_left)
    send(gb.at[0], gb.at[1], x_send.at[2], x_recv.at[2], at_x(1))
    send(gb.at[0], gb.at[2], x_send.at[3], x_recv.at[3], at_x(-1))
    send(st.at[0], st.at[1], x_send.at[4], x_recv.at[4], at_x(1))
    send(st.at[0], st.at[2], x_send.at[5], x_recv.at[5], at_x(-1))
    landed(qb.at[1], x_recv.at[0])
    send(qb.at[1], qb.at[3], x_send.at[6], x_recv.at[6], at_x(1))

    for d in (1, 2, 3, 4):
        landed(kbuf.at[4 - d, core], k_recv.at[4 - d, 0])
    near = pl.ds(other, 4)
    send(kbuf.at[near, core], kbuf.at[near, core], c_send.at[0], c_recv.at[0], partner)
    for d in (1, 2, 3):
        landed(vbuf.at[4, core, ys(d)], v_recv.at[4, ys(d)])
        landed(vbuf.at[pl.ds(0, 4), core, ys(d)], v_recv.at[5, ys(d)])
    send(vbuf.at[near, core], vbuf.at[near, core], c_send.at[1], c_recv.at[1], partner)
    for d in (1, 2, 3):
        landed(idq.at[lax.rem(x + 4 - d, 4)], x_recv.at[d + 9])

    pieces = []
    for y in range(NY):
        for col in range(4):
            tile = idq[col, y]
            pieces.append(jnp.broadcast_to(tile[:, 0:1], (8, 128)))
            pieces.append(jnp.broadcast_to(tile[:, 64:65], (8, 128)))
    ids_query = jnp.concatenate(pieces, axis=0).T[0:1, :]
    landed(kbuf.at[pl.ds(core, 4), other], c_recv.at[0])
    landed(vbuf.at[pl.ds(core, 4), other], c_recv.at[1])

    query_pos = core * ROWS + lax.broadcasted_iota(jnp.int32, (1, ROWS), 1)
    first = unit * 2 * ROWS

    def prepare(n, carry):
        block = core + n // NY
        y = n % NY
        j, c = lax.div(block, 2), lax.rem(block, 2)
        rows = pl.ds(pl.multiple_of(n * PIECE, PIECE), PIECE)
        keys = jnp.concatenate([kbuf[j, c, y, 0:16, :], kbuf[j, c, y, 16:32, :]], axis=1)
        vals = jnp.concatenate([vbuf[j, c, y, 0:16, :], vbuf[j, c, y, 16:32, :]], axis=1)
        kf[rows, :] = keys
        kh[rows, :], kl[rows, :] = halves(keys)
        vh[rows, :], vl[rows, :] = halves(vals)
        tile = kbuf[j, c, y, 32:40, :]
        ids = jnp.concatenate([tile[:, 0:1], tile[:, 64:65]], axis=0)
        key_pos = (block - 8) * ROWS + y * BAND + x * PIECE
        key_pos = key_pos + lax.broadcasted_iota(jnp.int32, (PIECE, ROWS), 0)
        apart = query_pos - key_pos
        allowed = (apart >= 0) & (apart < WIN) & (ids == ids_query) & (key_pos + first >= 0)
        bias[rows, :] = jnp.where(allowed, 0.0, -1e30)
        return carry

    lax.fori_loop(0, KEYS // PIECE, prepare, 0)
    kf[KEYS:PAD, :] = jnp.zeros((PAD - KEYS, 256), f32)
    sh[KEYS:PAD, :] = jnp.zeros((PAD - KEYS, ROWS), bf16)
    sl[KEYS:PAD, :] = jnp.zeros((PAD - KEYS, ROWS), bf16)
    for i in range(PAD // 128):
        cols = slice(i * 128, (i + 1) * 128)
        kth[:, cols], ktl[:, cols] = halves(kf[cols, :].T)

    TILE = 192

    def one_head(slot, is_first):
        even, odd = pl.ds(0, ROWS, stride=2), pl.ds(1, ROWS, stride=2)
        qh[...], ql[...] = halves(jnp.concatenate([qb[slot, even, :], qb[slot, odd, :]], axis=1) * 0.0625)
        gh[...], gl[...] = halves(jnp.concatenate([gb[slot, even, :], gb[slot, odd, :]], axis=1))
        norm, delta = st[slot, 0:1, :], st[slot, 1:2, :]
        for t in range(KEYS // TILE):
            rows = slice(t * TILE, (t + 1) * TILE)
            scores = dot3(kh[rows, :], kl[rows, :], qh[...], ql[...], 1)
            grads = dot3(vh[rows, :], vl[rows, :], gh[...], gl[...], 1)
            probs = jnp.exp(scores - norm + bias[rows, :])
            grads = probs * (grads - delta)
            p_high, p_low = halves(probs)
            s_high, s_low = halves(grads)
            sh[rows, :] = s_high
            sl[rows, :] = s_low
            out = pl.ds(pl.multiple_of(core * BAND + t * TILE, BAND), TILE)
            part_v = dot3(p_high, p_low, gh[...], gl[...], 0)
            part_k = dot3(s_high, s_low, qh[...], ql[...], 0)
            if is_first:
                acc_v[out, :] = part_v
                acc_k[out, :] = part_k
            else:
                acc_v[out, :] += part_v
                acc_k[out, :] += part_k
        dq_part[slot] = dot3(kth[...], ktl[...], sh[...], sl[...], 0)

    one_head(0, True)
    landed(gb.at[2], x_recv.at[3])
    send(gb.at[2], gb.at[3], x_send.at[7], x_recv.at[7], at_x(-1))
    landed(gb.at[1], x_recv.at[2])
    landed(st.at[1], x_recv.at[4])
    send(st.at[1], st.at[3], x_send.at[8], x_recv.at[8], at_x(1))
    one_head(1, False)
    send(dq_part.at[1], dq_in.at[0], x_send.at[13], x_recv.at[13], at_x(-1))
    landed(qb.at[2], x_recv.at[1])
    landed(st.at[2], x_recv.at[5])
    one_head(2, False)
    send(dq_part.at[2], dq_in.at[1], x_send.at[14], x_recv.at[14], at_x(1))
    landed(qb.at[3], x_recv.at[6])
    landed(gb.at[3], x_recv.at[7])
    landed(st.at[3], x_recv.at[8])
    one_head(3, False)
    send(dq_part.at[3], dq_in.at[2], x_send.at[15], x_recv.at[15], at_x(2))

    def band(ref, j, c):
        return ref.at[pl.ds(pl.multiple_of((j * 2 + c) * BAND, BAND), BAND)]

    def rows_of(j, c, y=0, count=BAND):
        return pl.ds(pl.multiple_of((j * 2 + c) * BAND + y * PIECE, PIECE), count)

    for i in range(4):
        j = core + i
        send(band(acc_v, j, other), core_v.at[i], c_send.at[2 + i], c_recv.at[2 + i], partner)
        send(band(acc_k, j, other), core_k.at[i], c_send.at[6 + i], c_recv.at[6 + i], partner)
    for i in range(4):
        j = other + i
        landed(core_v.at[i], c_recv.at[2 + i])
        acc_v[rows_of(j, core), :] += core_v[i]
    for d in (1, 2, 3, 4):
        send(band(acc_v, 4 - d, core), u_v.at[d - 1], r_send.at[d - 1], r_recv.at[d - 1], at_unit(-d))
    for i in range(4):
        j = other + i
        landed(core_k.at[i], c_recv.at[6 + i])
        acc_k[rows_of(j, core), :] += core_k[i]
    for d in (1, 2, 3):
        y = ys(d)
        for j in range(UNITS):
            sum_k[d, j] = acc_k[rows_of(j, core, y, PIECE), :]
        send(sum_k.at[d], y_k.at[d - 1], r_send.at[d + 3], r_recv.at[d + 3], at_y(d))

    total = acc_v[rows_of(4, core), :]
    for d in (1, 2, 3, 4):
        landed(u_v.at[d - 1], r_recv.at[d - 1])
        total = total + u_v[d - 1]
    sum_v[...] = total
    for d in (1, 2, 3):
        src = sum_v.at[pl.ds(pl.multiple_of(ys(d) * PIECE, PIECE), PIECE)]
        send(src, y_v.at[d - 1], r_send.at[d + 6], r_recv.at[d + 6], at_y(d))
    for d in (1, 2, 3):
        landed(y_k.at[d - 1], r_recv.at[d + 3])
    for j in range(UNITS):
        sum_k[0, j] = acc_k[rows_of(j, core, yh, PIECE), :] + y_k[0, j] + y_k[1, j] + y_k[2, j]
    for d in (1, 2, 3, 4):
        send(sum_k.at[0, 4 - d], u_k.at[d - 1], r_send.at[d + 9], r_recv.at[d + 9], at_unit(-d))

    for i in range(3):
        landed(dq_in.at[i], x_recv.at[13 + i])
    total_q = (dq_part[0] + dq_in[0] + dq_in[1] + dq_in[2]) * 0.0625
    total_q = total_q.T
    dq_out[pl.ds(0, ROWS, stride=2), :] = total_q[:, :128]
    dq_out[pl.ds(1, ROWS, stride=2), :] = total_q[:, 128:]

    total = sum_v[pl.ds(pl.multiple_of(yh * PIECE, PIECE), PIECE), :]
    for d in (1, 2, 3):
        landed(y_v.at[d - 1], r_recv.at[d + 6])
        total = total + y_v[d - 1]
    dv_out[...] = total
    total = sum_k[0, 4]
    for d in (1, 2, 3, 4):
        landed(u_k.at[d - 1], r_recv.at[d + 9])
        total = total + u_k[d - 1]
    dk_out[...] = total
    for copy in started:
        copy.wait_send()


def on_device(queries, key_rows, value_rows, forward_out, out_grad, log_norm, doc_ids):
    flat = (2 * ROWS, 128)
    vmem, dma = pltpu.VMEM, pltpu.SemaphoreType.DMA
    dq, dk, dv = pl.pallas_call(
        kernel,
        out_shape=(
            jax.ShapeDtypeStruct(flat, f32),
            jax.ShapeDtypeStruct((PIECE, 256), f32),
            jax.ShapeDtypeStruct((PIECE, 256), f32),
        ),
        in_specs=[pl.BlockSpec(memory_space=pl.ANY)] * 7,
        out_specs=(pl.BlockSpec(memory_space=pltpu.VMEM),) * 3,
        scratch_shapes=[
            vmem((4, *flat), f32), vmem((4, *flat), f32), vmem((4, 8, ROWS), f32), vmem(flat, f32),
            vmem((1, ROWS), f32), vmem((1, PIECE), jnp.int32), vmem((PIECE, 256), f32), vmem((PIECE, 256), f32),
            vmem((UNITS, 2, NY, 40, 128), f32), vmem((UNITS, 2, NY, 32, 128), f32), vmem((4, NY, 8, 128), f32),
            vmem((PAD, 256), f32), vmem((KEYS, 256), bf16), vmem((KEYS, 256), bf16),
            vmem((KEYS, 256), bf16), vmem((KEYS, 256), bf16), vmem((256, PAD), bf16), vmem((256, PAD), bf16),
            vmem((8, 128), f32), vmem((KEYS, ROWS), f32),
            vmem((ROWS, 256), bf16), vmem((ROWS, 256), bf16), vmem((ROWS, 256), bf16), vmem((ROWS, 256), bf16),
            vmem((PAD, ROWS), bf16), vmem((PAD, ROWS), bf16),
            vmem((10 * BAND, 256), f32), vmem((10 * BAND, 256), f32),
            vmem((4, BAND, 256), f32), vmem((4, BAND, 256), f32),
            vmem((3, UNITS, PIECE, 256), f32), vmem((4, PIECE, 256), f32), vmem((4, BAND, 256), f32),
            vmem((3, PIECE, 256), f32), vmem((4, UNITS, PIECE, 256), f32), vmem((BAND, 256), f32),
            vmem((4, 256, ROWS), f32), vmem((3, 256, ROWS), f32),
            dma((7,)), dma((16,)), dma((16,)), dma((7,)), dma((5, NY)), dma((10,)), dma((6, NY)),
            dma((10,)), dma((10,)), dma((14,)), dma((14,)),
        ],
        compiler_params=pltpu.CompilerParams(
            collective_id=0, has_side_effects=True, vmem_limit_bytes=60 * 2**20
        ),
    )(
        queries.reshape(flat), key_rows, value_rows, forward_out.reshape(flat), out_grad.reshape(flat),
        log_norm.reshape(1, ROWS), doc_ids.reshape(1, PIECE),
    )
    return dq.reshape(ROWS, 1, 256), dk, dv


def solution(mesh):
    in_specs = (
        P("seq", "head", None),
        P(("seq", "head"), None),
        P(("seq", "head"), None),
        P("seq", "head", None),
        P("seq", "head", None),
        P("seq", "head"),
        P(("seq", "head")),
    )
    out_specs = (P("seq", "head", None), P(("seq", "head"), None), P(("seq", "head"), None))
    return jax.shard_map(
        on_device, mesh=mesh, in_specs=in_specs, out_specs=out_specs, check_vma=False
    )
```

time: 366 us -> 76.8 us (0.21)
  the two profiles are of different devices: /device:TPU:704 before, /device:TPU:6 now
where the time goes in v1:
time: 76.8 us; the launch traced here: 76.6 us
  Pallas kernels  72.8 us (95%)
  local copies, waits for them, and re-layouts  3.17 us (4%)
    pallas_call x1, Pallas kernels, on_device(): pl.pallas_call(kernel, out_shape=(jax.ShapeDtypeStruct(flat, f32), jax.Sh...  72.8 us
    unnamed x7, local copies, waits for them, and re-layouts  3.17 us

profile of v1, /device:TPU:6, one launch (start us, length us, event | category | flops | bytes accessed | tf_op | source)
XLA Modules:
  0.0 76.6 jit_solution(8820241654832784399)
XLA Ops:
  0.6 72.8 %shard_map.94 = (f32[512,128]{1,0:T(8,128)}, f32[16,256]{1,0:T(8,128)}, f32[16,256]{1,0:T(8,128)}) custom-call(f32[512,128]{1,0:T(8,128)} %bitcast.6, f32[16,256]{1,0:T(8,128)} %k_hbm.1, f32[16,256]{1,0:T(8,128)} %v_hbm.1, f32[512,128]{1,0:T(8,128)} %bitcast.7, f32[512,128]{1,0:T(8,128)} %bitcast.8, f32[1,256]{1,0:T(1,128)} %bitcast.10, s32[1,16]{1,0:T(1,128)} %bitcast.11), custom_call_target="tpu_custom_call" | custom-call | tf_op jit(solution)/shard_map/pallas_call | solution.py:321
  73.4 0.0 copy-start.1
  73.4 1.8 %copy.14 = f32[256,1,256]{2,1,0:T(1,128)} copy(f32[256,1,256]{2,1,0:T(1,128)} %bitcast.9) | data formatting | bytes 524288
  75.3 0.0 copy-done.1
  75.3 0.0 copy-start
  75.3 0.6 copy.15
  75.9 0.1 copy-done
  76.0 0.6 copy.16
Async XLA Ops:
  73.4 1.9 %copy-start.1 = (f32[16,256]{1,0:T(8,128)S(1)}, f32[16,256]{1,0:T(8,128)}, u32[]{:S(2)}) copy-start(f32[16,256]{1,0:T(8,128)} %get-tuple-element.16) | copy-start | bytes 49156
  75.3 0.7 copy-start

commit v2 on v1

v2 whole, which is shorter than its diff:
```python
import functools

import jax
import jax.numpy as jnp
from jax import lax
from jax.experimental import pallas as pl
from jax.experimental.pallas import tpu as pltpu
from jax.sharding import PartitionSpec as P

MESH = pl.DeviceIdType.MESH
WIN = 2048
ROWS = 256
PIECE = 16
UNITS = 5
NY = 4
BAND = NY * PIECE
KEYS = 9 * BAND
PAD = 640
f32, bf16 = jnp.float32, jnp.bfloat16


def halves(value):
    high = value.astype(bf16)
    return high, (value - high.astype(f32)).astype(bf16)


def dot(a, b, b_dim):
    return lax.dot_general(a, b, (((1,), (b_dim,)), ((), ())), preferred_element_type=f32)


def dot3(a_high, a_low, b_high, b_low, b_dim):
    return dot(a_high, b_high, b_dim) + dot(a_high, b_low, b_dim) + dot(a_low, b_high, b_dim)


def kernel(
    q_hbm, k_hbm, v_hbm, o_hbm, g_hbm, norm_hbm, ids_hbm,
    dq_hbm, dk_hbm, dv_hbm,
    dq_out, dk_out, dv_out, qb, gb, st, fwd, norm_in, ids_in, k_in, v_in,
    kbuf, vbuf, idq,
    kf, kh, kl, vh, vl, kth, ktl, bias,
    qh, ql, gh, gl, sh, sl,
    acc_k, acc_v, core_k, core_v, y_k, u_k, u_v, y_v, sum_k, sum_v, dq_part, dq_in,
    in_sem, out_sem, x_send, x_recv, k_send, k_recv, v_send, v_recv, c_send, c_recv, r_send, r_recv,
):
    seq, head = lax.axis_index("seq"), lax.axis_index("head")
    n_seq = lax.axis_size("seq")
    unit, core = lax.div(seq, 2), lax.rem(seq, 2)
    n_unit = n_seq // 2
    yh, x = lax.div(head, 4), lax.rem(head, 4)
    other = 1 - core

    def at_unit(d):
        return (lax.rem(unit + d + n_unit, n_unit) * 2 + core, head)

    def at_y(d):
        return (seq, lax.rem(yh + d, NY) * 4 + x)

    def at_x(d):
        return (seq, yh * 4 + lax.rem(x + d + 4, 4))

    partner = (unit * 2 + other, head)

    def send(src, dst, s_sem, r_sem, to):
        copy = pltpu.make_async_remote_copy(
            src_ref=src, dst_ref=dst, send_sem=s_sem, recv_sem=r_sem, device_id=to, device_id_type=MESH
        )
        copy.start()
        started.append(copy)
        return copy

    def landed(dst, r_sem):
        pltpu.make_async_remote_copy(
            src_ref=dst, dst_ref=dst, send_sem=r_sem, recv_sem=r_sem, device_id=partner, device_id_type=MESH
        ).wait_recv()

    started = []

    loads = [
        pltpu.make_async_copy(src, dst, in_sem.at[i])
        for i, (src, dst) in enumerate(
            (
                (q_hbm, qb.at[0]), (k_hbm, k_in), (v_hbm, v_in), (ids_hbm, ids_in),
                (g_hbm, gb.at[0]), (o_hbm, fwd), (norm_hbm, norm_in),
            )
        )
    ]
    for load in loads:
        load.start()
    barrier = pltpu.get_barrier_semaphore()
    greeted = [at_x(1), at_x(-1), at_x(2), partner]
    greeted += [at_y(d) for d in (1, 2, 3)] + [at_unit(-d) for d in (1, 2, 3, 4)]
    for device in greeted:
        pl.semaphore_signal(barrier, inc=1, device_id=device, device_id_type=MESH)

    for load in loads[:4]:
        load.wait()
    ids_row = ids_in[...].astype(f32)
    across = lax.broadcasted_iota(jnp.int32, (8, PIECE), 1)
    down = lax.broadcasted_iota(jnp.int32, (8, PIECE), 0)
    ids_low = jnp.sum(jnp.where(across == down, ids_row, 0.0), axis=1, keepdims=True)
    ids_high = jnp.sum(jnp.where(across == down + 8, ids_row, 0.0), axis=1, keepdims=True)
    lane = lax.broadcasted_iota(jnp.int32, (8, 128), 1)
    ids_tile = jnp.where(lane < 64, ids_low, ids_high)
    mine_k = kbuf.at[4, core, 0]
    mine_v = vbuf.at[4, core, 0]
    kbuf[4, core, 0, 0:16, :] = k_in[:, :128]
    kbuf[4, core, 0, 16:32, :] = k_in[:, 128:]
    kbuf[4, core, 0, 32:40, :] = ids_tile
    vbuf[4, core, 0, 0:16, :] = v_in[:, :128]
    vbuf[4, core, 0, 16:32, :] = v_in[:, 128:]
    pl.semaphore_wait(barrier, len(greeted))

    q_right = send(qb.at[0], qb.at[1], x_send.at[0], x_recv.at[0], at_x(1))
    q_left = send(qb.at[0], qb.at[2], x_send.at[1], x_recv.at[1], at_x(-1))
    for d in (1, 2, 3):
        send(mine_k, kbuf.at[4, core, 4 - d], k_send.at[d - 1], k_recv.at[3 - d], at_y(d))
    for d in (1, 2, 3, 4):
        send(mine_v, vbuf.at[4 - d, core, 0], v_send.at[d - 1], v_recv.at[d - 1], at_unit(d))
    for d in (1, 2, 3, 4):
        send(mine_k, kbuf.at[4 - d, core, 0], k_send.at[d + 2], k_recv.at[d + 2], at_unit(d))
    for d in (1, 2, 3):
        send(mine_v, vbuf.at[4, core, 4 - d], v_send.at[d + 3], v_recv.at[d + 3], at_y(d))

    for load in loads[4:]:
        load.wait()
    product = gb[0] * fwd[...]
    fwd[...] = product
    folded = fwd[pl.ds(0, ROWS, stride=2), :] + fwd[pl.ds(1, ROWS, stride=2), :]
    st[0, 0:1, :] = norm_in[...]
    st[0, 1:2, :] = jnp.sum(folded.T, axis=0, keepdims=True)
    st[0, 2:8, :] = jnp.zeros((6, ROWS), f32)

    for r in (1, 2, 3):
        landed(kbuf.at[4, core, r], k_recv.at[r - 1])
    along = pl.ds(1, 3)
    for d in (1, 2, 3, 4):
        send(kbuf.at[4, core, along], kbuf.at[4 - d, core, along], k_send.at[d + 6], k_recv.at[d + 6], at_unit(d))
    for d in (1, 2, 3, 4):
        landed(vbuf.at[4 - d, core, 0], v_recv.at[d - 1])
    past = pl.ds(0, 4)
    for d in (1, 2, 3):
        send(vbuf.at[past, core, 0], vbuf.at[past, core, 4 - d], v_send.at[d + 6], v_recv.at[d + 6], at_y(d))
    idq[pl.ds(x, 1)] = kbuf[4, core, :, 32:40, :][None]
    for d in (1, 2, 3):
        send(idq.at[x], idq.at[x], x_send.at[d + 9], x_recv.at[d + 9], at_x(d))
    q_right.wait_send()
    q_left.wait_send()
    started.remove(q_right)
    started.remove(q_left)
    send(gb.at[0], gb.at[1], x_send.at[2], x_recv.at[2], at_x(1))
    send(gb.at[0], gb.at[2], x_send.at[3], x_recv.at[3], at_x(-1))
    send(st.at[0], st.at[1], x_send.at[4], x_recv.at[4], at_x(1))
    send(st.at[0], st.at[2], x_send.at[5], x_recv.at[5], at_x(-1))
    landed(qb.at[1], x_recv.at[0])
    send(qb.at[1], qb.at[3], x_send.at[6], x_recv.at[6], at_x(1))

    for d in (1, 2, 3):
        landed(idq.at[lax.rem(x + 4 - d, 4)], x_recv.at[d + 9])
    pieces = []
    for y in range(NY):
        for col in range(4):
            tile = idq[col, lax.rem(y + NY - yh, NY)]
            pieces.append(jnp.broadcast_to(tile[:, 0:1], (8, 128)))
            pieces.append(jnp.broadcast_to(tile[:, 64:65], (8, 128)))
    ids_query = jnp.concatenate(pieces, axis=0).T[0:1, :]
    query_pos = core * ROWS + lax.broadcasted_iota(jnp.int32, (1, ROWS), 1)
    first = unit * 2 * ROWS
    row = lax.broadcasted_iota(jnp.int32, (BAND, 1), 0)
    row_pos = lax.rem(yh + row // PIECE, NY) * BAND + x * PIECE + row % PIECE

    def prepare(band, j, c):
        rows = slice(band * BAND, (band + 1) * BAND)

        def wide(ref, lo):
            return ref[j, c, :, lo : lo + PIECE, :].reshape(BAND, 128)

        keys = jnp.concatenate([wide(kbuf, 0), wide(kbuf, PIECE)], axis=1)
        vals = jnp.concatenate([wide(vbuf, 0), wide(vbuf, PIECE)], axis=1)
        kf[rows, :] = keys
        kh[rows, :], kl[rows, :] = halves(keys)
        vh[rows, :], vl[rows, :] = halves(vals)
        tiles = kbuf[j, c, :, 32:40, :]
        ids = jnp.concatenate([tiles[:, :, 0:1], tiles[:, :, 64:65]], axis=1).reshape(BAND, 1)
        key_pos = row_pos + (core + band - 8) * ROWS
        apart = query_pos - key_pos
        allowed = (apart >= 0) & (apart < WIN) & (ids == ids_query) & (key_pos + first >= 0)
        bias[rows, :] = jnp.where(allowed, 0.0, -1e30)

    kf[KEYS:PAD, :] = jnp.zeros((PAD - KEYS, 256), f32)
    sh[KEYS:PAD, :] = jnp.zeros((PAD - KEYS, ROWS), bf16)
    sl[KEYS:PAD, :] = jnp.zeros((PAD - KEYS, ROWS), bf16)

    near = pl.ds(other, 4)
    for d in (1, 2, 3):
        landed(vbuf.at[4, core, 4 - d], v_recv.at[d + 3])
        landed(vbuf.at[past, core, 4 - d], v_recv.at[d + 6])
    send(vbuf.at[near, core], vbuf.at[near, core], c_send.at[1], c_recv.at[1], partner)
    for d in (1, 2, 3, 4):
        landed(kbuf.at[4 - d, core, 0], k_recv.at[d + 2])
        landed(kbuf.at[4 - d, core, along], k_recv.at[d + 6])
    send(kbuf.at[near, core], kbuf.at[near, core], c_send.at[0], c_recv.at[0], partner)
    for j in range(UNITS):
        prepare(2 * j, j, core)
    landed(gb.at[2], x_recv.at[3])
    send(gb.at[2], gb.at[3], x_send.at[7], x_recv.at[7], at_x(-1))
    landed(st.at[1], x_recv.at[4])
    send(st.at[1], st.at[3], x_send.at[8], x_recv.at[8], at_x(1))
    landed(vbuf.at[pl.ds(core, 4), other], c_recv.at[1])
    landed(kbuf.at[pl.ds(core, 4), other], c_recv.at[0])
    for i in range(4):
        prepare(2 * i + 1, core + i, other)
    for i in range(PAD // 128):
        cols = slice(i * 128, (i + 1) * 128)
        kth[:, cols], ktl[:, cols] = halves(kf[cols, :].T)

    TILE = 192

    def one_head(slot, is_first):
        even, odd = pl.ds(0, ROWS, stride=2), pl.ds(1, ROWS, stride=2)
        qh[...], ql[...] = halves(jnp.concatenate([qb[slot, even, :], qb[slot, odd, :]], axis=1) * 0.0625)
        gh[...], gl[...] = halves(jnp.concatenate([gb[slot, even, :], gb[slot, odd, :]], axis=1))
        norm, delta = st[slot, 0:1, :], st[slot, 1:2, :]
        for t in range(KEYS // TILE):
            rows = slice(t * TILE, (t + 1) * TILE)
            scores = dot3(kh[rows, :], kl[rows, :], qh[...], ql[...], 1)
            grads = dot3(vh[rows, :], vl[rows, :], gh[...], gl[...], 1)
            probs = jnp.exp(scores - norm + bias[rows, :])
            grads = probs * (grads - delta)
            p_high, p_low = halves(probs)
            s_high, s_low = halves(grads)
            sh[rows, :] = s_high
            sl[rows, :] = s_low
            part_v = dot3(p_high, p_low, gh[...], gl[...], 0)
            part_k = dot3(s_high, s_low, qh[...], ql[...], 0)
            for i in range(TILE // BAND):
                block = core + t * (TILE // BAND) + i
                j, c = lax.div(block, 2), lax.rem(block, 2)
                part = slice(i * BAND, (i + 1) * BAND)
                if is_first:
                    acc_v[j, c] = part_v[part]
                    acc_k[j, c] = part_k[part]
                else:
                    acc_v[j, c] += part_v[part]
                    acc_k[j, c] += part_k[part]
        dq_part[slot] = dot3(kth[...], ktl[...], sh[...], sl[...], 0)

    one_head(0, True)
    landed(gb.at[1], x_recv.at[2])
    one_head(1, False)
    send(dq_part.at[1], dq_in.at[0], x_send.at[13], x_recv.at[13], at_x(-1))
    landed(qb.at[2], x_recv.at[1])
    landed(st.at[2], x_recv.at[5])
    one_head(2, False)
    send(dq_part.at[2], dq_in.at[1], x_send.at[14], x_recv.at[14], at_x(1))
    landed(qb.at[3], x_recv.at[6])
    landed(gb.at[3], x_recv.at[7])
    landed(st.at[3], x_recv.at[8])
    one_head(3, False)

    share = pl.ds(core, 4)
    send(acc_v.at[share, other], core_v, c_send.at[2], c_recv.at[2], partner)
    send(acc_k.at[share, other], core_k, c_send.at[3], c_recv.at[3], partner)
    send(dq_part.at[3], dq_in.at[2], x_send.at[15], x_recv.at[15], at_x(2))
    landed(core_v, c_recv.at[2])
    for i in range(4):
        acc_v[other + i, core] += core_v[i]
    for d in (4, 3, 2, 1):
        send(acc_v.at[4 - d, core], u_v.at[d - 1], r_send.at[d - 1], r_recv.at[d - 1], at_unit(-d))
    landed(core_k, c_recv.at[3])
    for i in range(4):
        acc_k[other + i, core] += core_k[i]
    for r in (2, 1, 3):
        src = acc_k.at[:, core, pl.ds(r * PIECE, PIECE)]
        send(src, y_k.at[r - 1], r_send.at[r + 3], r_recv.at[r + 3], at_y(r))

    total = acc_v[4, core]
    for d in (1, 2, 3, 4):
        landed(u_v.at[d - 1], r_recv.at[d - 1])
        total = total + u_v[d - 1]
    sum_v[...] = total
    for r in (2, 1, 3):
        src = sum_v.at[pl.ds(r * PIECE, PIECE)]
        send(src, y_v.at[r - 1], r_send.at[r + 6], r_recv.at[r + 6], at_y(r))
    for r in (1, 2, 3):
        landed(y_k.at[r - 1], r_recv.at[r + 3])
    for j in range(UNITS):
        sum_k[j] = acc_k[j, core, :PIECE] + y_k[0, j] + y_k[1, j] + y_k[2, j]
    for d in (4, 3, 2, 1):
        send(sum_k.at[4 - d], u_k.at[d - 1], r_send.at[d + 9], r_recv.at[d + 9], at_unit(-d))

    for i in range(3):
        landed(dq_in.at[i], x_recv.at[13 + i])
    total_q = (dq_part[0] + dq_in[0] + dq_in[1] + dq_in[2]) * 0.0625
    total_q = total_q.T
    dq_out[pl.ds(0, ROWS, stride=2), :] = total_q[:, :128]
    dq_out[pl.ds(1, ROWS, stride=2), :] = total_q[:, 128:]
    stores = [pltpu.make_async_copy(dq_out, dq_hbm, out_sem.at[0])]
    stores[0].start()

    total = sum_v[:PIECE, :]
    for r in (1, 2, 3):
        landed(y_v.at[r - 1], r_recv.at[r + 6])
        total = total + y_v[r - 1]
    dv_out[...] = total
    stores.append(pltpu.make_async_copy(dv_out, dv_hbm, out_sem.at[1]))
    stores[1].start()
    total = sum_k[4]
    for d in (1, 2, 3, 4):
        landed(u_k.at[d - 1], r_recv.at[d + 9])
        total = total + u_k[d - 1]
    dk_out[...] = total
    stores.append(pltpu.make_async_copy(dk_out, dk_hbm, out_sem.at[2]))
    stores[2].start()
    for store in stores:
        store.wait()
    for copy in started:
        copy.wait_send()


def hand_over(dq_in, dk_in, dv_in, dq_out, dk_out, dv_out):
    dq_out[...] = dq_in[...]
    dk_out[...] = dk_in[...]
    dv_out[...] = dv_in[...]


def on_device(queries, key_rows, value_rows, forward_out, out_grad, log_norm, doc_ids):
    flat = (2 * ROWS, 128)
    vmem, dma = pltpu.VMEM, pltpu.SemaphoreType.DMA
    dq, dk, dv = pl.pallas_call(
        kernel,
        out_shape=(
            jax.ShapeDtypeStruct(flat, f32),
            jax.ShapeDtypeStruct((PIECE, 256), f32),
            jax.ShapeDtypeStruct((PIECE, 256), f32),
        ),
        in_specs=[pl.BlockSpec(memory_space=pl.ANY)] * 7,
        out_specs=(pl.BlockSpec(memory_space=pl.ANY),) * 3,
        scratch_shapes=[
            vmem(flat, f32), vmem((PIECE, 256), f32), vmem((PIECE, 256), f32),
            vmem((4, *flat), f32), vmem((4, *flat), f32), vmem((4, 8, ROWS), f32), vmem(flat, f32),
            vmem((1, ROWS), f32), vmem((1, PIECE), jnp.int32), vmem((PIECE, 256), f32), vmem((PIECE, 256), f32),
            vmem((UNITS, 2, NY, 40, 128), f32), vmem((UNITS, 2, NY, 32, 128), f32), vmem((4, NY, 8, 128), f32),
            vmem((PAD, 256), f32), vmem((KEYS, 256), bf16), vmem((KEYS, 256), bf16),
            vmem((KEYS, 256), bf16), vmem((KEYS, 256), bf16), vmem((256, PAD), bf16), vmem((256, PAD), bf16),
            vmem((KEYS, ROWS), f32),
            vmem((ROWS, 256), bf16), vmem((ROWS, 256), bf16), vmem((ROWS, 256), bf16), vmem((ROWS, 256), bf16),
            vmem((PAD, ROWS), bf16), vmem((PAD, ROWS), bf16),
            vmem((UNITS, 2, BAND, 256), f32), vmem((UNITS, 2, BAND, 256), f32),
            vmem((4, BAND, 256), f32), vmem((4, BAND, 256), f32),
            vmem((3, UNITS, PIECE, 256), f32), vmem((4, PIECE, 256), f32), vmem((4, BAND, 256), f32),
            vmem((3, PIECE, 256), f32), vmem((UNITS, PIECE, 256), f32), vmem((BAND, 256), f32),
            vmem((4, 256, ROWS), f32), vmem((3, 256, ROWS), f32),
            dma((7,)), dma((3,)), dma((16,)), dma((16,)), dma((11,)), dma((11,)), dma((10,)), dma((10,)),
            dma((4,)), dma((4,)), dma((14,)), dma((14,)),
        ],
        compiler_params=pltpu.CompilerParams(
            collective_id=0, has_side_effects=True, vmem_limit_bytes=60 * 2**20
        ),
    )(
        queries.reshape(flat), key_rows, value_rows, forward_out.reshape(flat), out_grad.reshape(flat),
        log_norm.reshape(1, ROWS), doc_ids.reshape(1, PIECE),
    )
    dq, dk, dv = pl.pallas_call(
        hand_over,
        out_shape=tuple(jax.ShapeDtypeStruct(a.shape, a.dtype) for a in (dq, dk, dv)),
        in_specs=[pl.BlockSpec(memory_space=pltpu.VMEM)] * 3,
        out_specs=(pl.BlockSpec(memory_space=pltpu.VMEM),) * 3,
    )(dq, dk, dv)
    return dq.reshape(ROWS, 1, 256), dk, dv


def solution(mesh):
    in_specs = (
        P("seq", "head", None),
        P(("seq", "head"), None),
        P(("seq", "head"), None),
        P("seq", "head", None),
        P("seq", "head", None),
        P("seq", "head"),
        P(("seq", "head")),
    )
    out_specs = (P("seq", "head", None), P(("seq", "head"), None), P(("seq", "head"), None))
    return jax.shard_map(
        on_device, mesh=mesh, in_specs=in_specs, out_specs=out_specs, check_vma=False
    )
```

time: 76.8 us -> 65.2 us (0.85)
  the two profiles are of different devices: /device:TPU:6 before, /device:TPU:8 now
where the time goes in v2:
time: 65.2 us; the launch traced here: 65 us
  Pallas kernels  64.4 us (99%)
    pallas_call x1, Pallas kernels, on_device(): pl.pallas_call(kernel, out_shape=(jax.ShapeDtypeStruct(flat, f32), jax.Sh...  62.7 us
    pallas_call x1, Pallas kernels, on_device(): pl.pallas_call(hand_over, out_shape=tuple((jax.ShapeDtypeStruct(a.shape,...  1.69 us

profile of v2, /device:TPU:8, one launch (start us, length us, event | category | flops | bytes accessed | tf_op | source)
XLA Modules:
  0.0 65.0 jit_solution(13061152064832301770)
XLA Ops:
  0.6 62.7 %shard_map.94 = (f32[512,128]{1,0:T(8,128)}, f32[16,256]{1,0:T(8,128)}, f32[16,256]{1,0:T(8,128)}) custom-call(f32[512,128]{1,0:T(8,128)} %bitcast.6, f32[16,256]{1,0:T(8,128)} %k_hbm.1, f32[16,256]{1,0:T(8,128)} %v_hbm.1, f32[512,128]{1,0:T(8,128)} %bitcast.7, f32[512,128]{1,0:T(8,128)} %bitcast.8, f32[1,256]{1,0:T(1,128)} %bitcast.9, s32[1,16]{1,0:T(1,128)} %bitcast.10), custom_call_target="tpu_custom_call" | custom-call | tf_op jit(solution)/shard_map/pallas_call | solution.py:329
  63.3 1.7 %shard_map.95 = (f32[512,128]{1,0:T(8,128)}, f32[16,256]{1,0:T(8,128)}, f32[16,256]{1,0:T(8,128)}) custom-call(f32[512,128]{1,0:T(8,128)} %get-tuple-element.9.dq_in, f32[16,256]{1,0:T(8,128)} %get-tuple-element.10.dk_in, f32[16,256]{1,0:T(8,128)} %get-tuple-element.11.dv_in), custom_call_target="tpu_custom_call" | custom-call | tf_op jit(solution)/shard_map/pallas_call | solution.py:363

commit v3 on v2

--- a/solution.py
+++ b/solution.py
@@ -29,7 +29,9 @@
 
 
 def dot3(a_high, a_low, b_high, b_low, b_dim):
-    return dot(a_high, b_high, b_dim) + dot(a_high, b_low, b_dim) + dot(a_low, b_high, b_dim)
+    left = jnp.concatenate([a_high, a_high, a_low], axis=1)
+    right = jnp.concatenate([b_high, b_low, b_high], axis=b_dim)
+    return dot(left, right, b_dim)
 
 
 def kernel(
@@ -40,7 +42,7 @@
     kf, kh, kl, vh, vl, kth, ktl, bias,
     qh, ql, gh, gl, sh, sl,
     acc_k, acc_v, core_k, core_v, y_k, u_k, u_v, y_v, sum_k, sum_v, dq_part, dq_in,
-    in_sem, out_sem, x_send, x_recv, k_send, k_recv, v_send, v_recv, c_send, c_recv, r_send, r_recv,
+    in_sem, out_sem, x_send, x_recv, k_send, k_recv, v_send, v_recv, c_send, c_recv, r_send, r_recv, u_send, u_recv, y_send, y_recv,
 ):
     seq, head = lax.axis_index("seq"), lax.axis_index("head")
     n_seq = lax.axis_size("seq")
@@ -213,7 +215,7 @@
         cols = slice(i * 128, (i + 1) * 128)
         kth[:, cols], ktl[:, cols] = halves(kf[cols, :].T)
 
-    TILE = 192
+    TILE = 576
 
     def one_head(slot, is_first):
         even, odd = pl.ds(0, ROWS, stride=2), pl.ds(1, ROWS, stride=2)
@@ -242,15 +244,20 @@
                 else:
                     acc_v[j, c] += part_v[part]
                     acc_k[j, c] += part_k[part]
+
+    def head_queries(slot):
         dq_part[slot] = dot3(kth[...], ktl[...], sh[...], sl[...], 0)
 
     one_head(0, True)
+    head_queries(0)
     landed(gb.at[1], x_recv.at[2])
     one_head(1, False)
+    head_queries(1)
     send(dq_part.at[1], dq_in.at[0], x_send.at[13], x_recv.at[13], at_x(-1))
     landed(qb.at[2], x_recv.at[1])
     landed(st.at[2], x_recv.at[5])
     one_head(2, False)
+    head_queries(2)
     send(dq_part.at[2], dq_in.at[1], x_send.at[14], x_recv.at[14], at_x(1))
     landed(qb.at[3], x_recv.at[6])
     landed(gb.at[3], x_recv.at[7])
@@ -260,33 +267,57 @@
     share = pl.ds(core, 4)
     send(acc_v.at[share, other], core_v, c_send.at[2], c_recv.at[2], partner)
     send(acc_k.at[share, other], core_k, c_send.at[3], c_recv.at[3], partner)
+    head_queries(3)
     send(dq_part.at[3], dq_in.at[2], x_send.at[15], x_recv.at[15], at_x(2))
+
+    def piece(r):
+        return pl.ds(r * PIECE, PIECE)
+
+    def values_on(r):
+        for d in (4, 3, 2, 1):
+            i = 4 * r + d - 1
+            send(acc_v.at[4 - d, core, piece(r)], u_v.at[d - 1, piece(r)], u_send.at[i], u_recv.at[i], at_unit(-d))
+
+    def keys_on(j):
+        for r in (2, 1, 3):
+            i = 3 * j + r - 1
+            send(acc_k.at[j, core, piece(r)], y_k.at[r - 1, j], y_send.at[i], y_recv.at[i], at_y(r))
+
+    def values_total(r):
+        total = acc_v[4, core, piece(r)]
+        for d in (4, 3, 2, 1):
+            landed(u_v.at[d - 1, piece(r)], u_recv.at[4 * r + d - 1])
+            total = total + u_v[d - 1, piece(r)]
+        return total
+
+    def keys_total(j):
+        total = acc_k[j, core, :PIECE]
+        for r in (2, 1, 3):
+            landed(y_k.at[r - 1, j], y_recv.at[3 * j + r - 1])
+            total = total + y_k[r - 1, j]
+        return total
+
     landed(core_v, c_recv.at[2])
     for i in range(4):
         acc_v[other + i, core] += core_v[i]
-    for d in (4, 3, 2, 1):
-        send(acc_v.at[4 - d, core], u_v.at[d - 1], r_send.at[d - 1], r_recv.at[d - 1], at_unit(-d))
+    values_on(2)
     landed(core_k, c_recv.at[3])
     for i in range(4):
         acc_k[other + i, core] += core_k[i]
-    for r in (2, 1, 3):
-        src = acc_k.at[:, core, pl.ds(r * PIECE, PIECE)]
-        send(src, y_k.at[r - 1], r_send.at[r + 3], r_recv.at[r + 3], at_y(r))
-
-    total = acc_v[4, core]
-    for d in (1, 2, 3, 4):
-        landed(u_v.at[d - 1], r_recv.at[d - 1])
-        total = total + u_v[d - 1]
-    sum_v[...] = total
-    for r in (2, 1, 3):
-        src = sum_v.at[pl.ds(r * PIECE, PIECE)]
-        send(src, y_v.at[r - 1], r_send.at[r + 6], r_recv.at[r + 6], at_y(r))
-    for r in (1, 2, 3):
-        landed(y_k.at[r - 1], r_recv.at[r + 3])
-    for j in range(UNITS):
-        sum_k[j] = acc_k[j, core, :PIECE] + y_k[0, j] + y_k[1, j] + y_k[2, j]
-    for d in (4, 3, 2, 1):
-        send(sum_k.at[4 - d], u_k.at[d - 1], r_send.at[d + 9], r_recv.at[d + 9], at_unit(-d))
+    keys_on(0)
+    values_on(1)
+    keys_on(1)
+    values_on(3)
+    keys_on(2)
+    keys_on(3)
+    values_on(0)
+    keys_on(4)
+    for r, j in ((2, 0), (1, 1), (3, 2), (None, 3)):
+        if r is not None:
+            sum_v[piece(r), :] = values_total(r)
+            send(sum_v.at[piece(r)], y_v.at[r - 1], r_send.at[r - 1], r_recv.at[r - 1], at_y(r))
+        sum_k[j] = keys_total(j)
+        send(sum_k.at[j], u_k.at[3 - j], r_send.at[6 - j], r_recv.at[6 - j], at_unit(j - 4))
 
     for i in range(3):
         landed(dq_in.at[i], x_recv.at[13 + i])
@@ -297,16 +328,16 @@
     stores = [pltpu.make_async_copy(dq_out, dq_hbm, out_sem.at[0])]
     stores[0].start()
 
-    total = sum_v[:PIECE, :]
+    total = values_total(0)
     for r in (1, 2, 3):
-        landed(y_v.at[r - 1], r_recv.at[r + 6])
+        landed(y_v.at[r - 1], r_recv.at[r - 1])
         total = total + y_v[r - 1]
     dv_out[...] = total
     stores.append(pltpu.make_async_copy(dv_out, dv_hbm, out_sem.at[1]))
     stores[1].start()
-    total = sum_k[4]
-    for d in (1, 2, 3, 4):
-        landed(u_k.at[d - 1], r_recv.at[d + 9])
+    total = keys_total(4)
+    for d in (1, 2, 3, 4):
+        landed(u_k.at[d - 1], r_recv.at[d + 2])
         total = total + u_k[d - 1]
     dk_out[...] = total
     stores.append(pltpu.make_async_copy(dk_out, dk_hbm, out_sem.at[2]))
@@ -351,7 +382,7 @@
             vmem((3, PIECE, 256), f32), vmem((UNITS, PIECE, 256), f32), vmem((BAND, 256), f32),
             vmem((4, 256, ROWS), f32), vmem((3, 256, ROWS), f32),
             dma((7,)), dma((3,)), dma((16,)), dma((16,)), dma((11,)), dma((11,)), dma((10,)), dma((10,)),
-            dma((4,)), dma((4,)), dma((14,)), dma((14,)),
+            dma((4,)), dma((4,)), dma((7,)), dma((7,)), dma((16,)), dma((16,)), dma((15,)), dma((15,)),
         ],
         compiler_params=pltpu.CompilerParams(
             collective_id=0, has_side_effects=True, vmem_limit_bytes=60 * 2**20

time: 65.2 us -> 61.7 us (0.946)
  Pallas kernels: 64.4 us -> 60.9 us
    pallas_call x1, Pallas kernels: 62.7 us -> 59.2 us  [on_device(): pl.pallas_call(kernel, out_shape=(jax.ShapeDtypeStruct(flat, f32), jax.Sh...]
where the time goes in v3:
time: 61.7 us; the launch traced here: 61.5 us
  Pallas kernels  60.9 us (99%)
  between operations  0.64 us (1%)
    pallas_call x1, Pallas kernels, on_device(): pl.pallas_call(kernel, out_shape=(jax.ShapeDtypeStruct(flat, f32), jax.Sh...  59.2 us
    pallas_call x1, Pallas kernels, on_device(): pl.pallas_call(hand_over, out_shape=tuple((jax.ShapeDtypeStruct(a.shape,...  1.69 us

profile of v3, /device:TPU:8, one launch (start us, length us, event | category | flops | bytes accessed | tf_op | source)
XLA Modules:
  0.0 61.5 jit_solution(4156547203020165594)
XLA Ops:
  0.6 59.2 %shard_map.94 = (f32[512,128]{1,0:T(8,128)}, f32[16,256]{1,0:T(8,128)}, f32[16,256]{1,0:T(8,128)}) custom-call(f32[512,128]{1,0:T(8,128)} %bitcast.6, f32[16,256]{1,0:T(8,128)} %k_hbm.1, f32[16,256]{1,0:T(8,128)} %v_hbm.1, f32[512,128]{1,0:T(8,128)} %bitcast.7, f32[512,128]{1,0:T(8,128)} %bitcast.8, f32[1,256]{1,0:T(1,128)} %bitcast.9, s32[1,16]{1,0:T(1,128)} %bitcast.10), custom_call_target="tpu_custom_call" | custom-call | tf_op jit(solution)/shard_map/pallas_call | solution.py:360
  59.8 1.7 %shard_map.95 = (f32[512,128]{1,0:T(8,128)}, f32[16,256]{1,0:T(8,128)}, f32[16,256]{1,0:T(8,128)}) custom-call(f32[512,128]{1,0:T(8,128)} %get-tuple-element.9.dq_in, f32[16,256]{1,0:T(8,128)} %get-tuple-element.10.dk_in, f32[16,256]{1,0:T(8,128)} %get-tuple-element.11.dv_in), custom_call_target="tpu_custom_call" | custom-call | tf_op jit(solution)/shard_map/pallas_call | solution.py:394

commit v4 on v3

--- a/solution.py
+++ b/solution.py
@@ -156,6 +156,13 @@
     landed(qb.at[1], x_recv.at[0])
     send(qb.at[1], qb.at[3], x_send.at[6], x_recv.at[6], at_x(1))
 
+    def split(slot):
+        even, odd = pl.ds(0, ROWS, stride=2), pl.ds(1, ROWS, stride=2)
+        qh[...], ql[...] = halves(jnp.concatenate([qb[slot, even, :], qb[slot, odd, :]], axis=1) * 0.0625)
+        gh[...], gl[...] = halves(jnp.concatenate([gb[slot, even, :], gb[slot, odd, :]], axis=1))
+
+    split(0)
+
     for d in (1, 2, 3):
         landed(idq.at[lax.rem(x + 4 - d, 4)], x_recv.at[d + 9])
     pieces = []
@@ -189,8 +196,8 @@
         bias[rows, :] = jnp.where(allowed, 0.0, -1e30)
 
     kf[KEYS:PAD, :] = jnp.zeros((PAD - KEYS, 256), f32)
-    sh[KEYS:PAD, :] = jnp.zeros((PAD - KEYS, ROWS), bf16)
-    sl[KEYS:PAD, :] = jnp.zeros((PAD - KEYS, ROWS), bf16)
+    sh[:, KEYS:PAD, :] = jnp.zeros((4, PAD - KEYS, ROWS), bf16)
+    sl[:, KEYS:PAD, :] = jnp.zeros((4, PAD - KEYS, ROWS), bf16)
 
     near = pl.ds(other, 4)
     for d in (1, 2, 3):
@@ -218,9 +225,8 @@
     TILE = 576
 
     def one_head(slot, is_first):
-        even, odd = pl.ds(0, ROWS, stride=2), pl.ds(1, ROWS, stride=2)
-        qh[...], ql[...] = halves(jnp.concatenate([qb[slot, even, :], qb[slot, odd, :]], axis=1) * 0.0625)
-        gh[...], gl[...] = halves(jnp.concatenate([gb[slot, even, :], gb[slot, odd, :]], axis=1))
+        if slot:
+            split(slot)
         norm, delta = st[slot, 0:1, :], st[slot, 1:2, :]
         for t in range(KEYS // TILE):
             rows = slice(t * TILE, (t + 1) * TILE)
@@ -230,8 +236,8 @@
             grads = probs * (grads - delta)
             p_high, p_low = halves(probs)
             s_high, s_low = halves(grads)
-            sh[rows, :] = s_high
-            sl[rows, :] = s_low
+            sh[slot, rows, :] = s_high
+            sl[slot, rows, :] = s_low
             part_v = dot3(p_high, p_low, gh[...], gl[...], 0)
             part_k = dot3(s_high, s_low, qh[...], ql[...], 0)
             for i in range(TILE // BAND):
@@ -246,10 +252,9 @@
                     acc_k[j, c] += part_k[part]
 
     def head_queries(slot):
-        dq_part[slot] = dot3(kth[...], ktl[...], sh[...], sl[...], 0)
+        dq_part[slot] = dot3(kth[...], ktl[...], sh[slot], sl[slot], 0)
 
     one_head(0, True)
-    head_queries(0)
     landed(gb.at[1], x_recv.at[2])
     one_head(1, False)
     head_queries(1)
@@ -312,6 +317,7 @@
     keys_on(3)
     values_on(0)
     keys_on(4)
+    head_queries(0)
     for r, j in ((2, 0), (1, 1), (3, 2), (None, 3)):
         if r is not None:
             sum_v[piece(r), :] = values_total(r)
@@ -375,7 +381,7 @@
             vmem((KEYS, 256), bf16), vmem((KEYS, 256), bf16), vmem((256, PAD), bf16), vmem((256, PAD), bf16),
             vmem((KEYS, ROWS), f32),
             vmem((ROWS, 256), bf16), vmem((ROWS, 256), bf16), vmem((ROWS, 256), bf16), vmem((ROWS, 256), bf16),
-            vmem((PAD, ROWS), bf16), vmem((PAD, ROWS), bf16),
+            vmem((4, PAD, ROWS), bf16), vmem((4, PAD, ROWS), bf16),
             vmem((UNITS, 2, BAND, 256), f32), vmem((UNITS, 2, BAND, 256), f32),
             vmem((4, BAND, 256), f32), vmem((4, BAND, 256), f32),
             vmem((3, UNITS, PIECE, 256), f32), vmem((4, PIECE, 256), f32), vmem((4, BAND, 256), f32),

time: 61.7 us -> 61.7 us (level)
  the two profiles are of different devices: /device:TPU:8 before, /device:TPU:10 now
where the time goes in v4:
time: 61.7 us; the launch traced here: 61.6 us
  Pallas kernels  60.9 us (99%)
  between operations  0.64 us (1%)
    pallas_call x1, Pallas kernels, on_device(): pl.pallas_call(kernel, out_shape=(jax.ShapeDtypeStruct(flat, f32), jax.Sh...  59.2 us
    pallas_call x1, Pallas kernels, on_device(): pl.pallas_call(hand_over, out_shape=tuple((jax.ShapeDtypeStruct(a.shape,...  1.69 us

profile of v4, /device:TPU:10, one launch (start us, length us, event | category | flops | bytes accessed | tf_op | source)
XLA Modules:
  0.0 61.6 jit_solution(12747095087672264644)
XLA Ops:
  0.6 59.2 %shard_map.94 = (f32[512,128]{1,0:T(8,128)}, f32[16,256]{1,0:T(8,128)}, f32[16,256]{1,0:T(8,128)}) custom-call(f32[512,128]{1,0:T(8,128)} %bitcast.6, f32[16,256]{1,0:T(8,128)} %k_hbm.1, f32[16,256]{1,0:T(8,128)} %v_hbm.1, f32[512,128]{1,0:T(8,128)} %bitcast.7, f32[512,128]{1,0:T(8,128)} %bitcast.8, f32[1,256]{1,0:T(1,128)} %bitcast.9, s32[1,16]{1,0:T(1,128)} %bitcast.10), custom_call_target="tpu_custom_call" | custom-call | tf_op jit(solution)/shard_map/pallas_call | solution.py:366
  59.9 1.7 %shard_map.95 = (f32[512,128]{1,0:T(8,128)}, f32[16,256]{1,0:T(8,128)}, f32[16,256]{1,0:T(8,128)}) custom-call(f32[512,128]{1,0:T(8,128)} %get-tuple-element.9.dq_in, f32[16,256]{1,0:T(8,128)} %get-tuple-element.10.dk_in, f32[16,256]{1,0:T(8,128)} %get-tuple-element.11.dv_in), custom_call_target="tpu_custom_call" | custom-call | tf_op jit(solution)/shard_map/pallas_call | solution.py:400
